TPU v7x, 32 devices: a whole 2x2x4 slice. The times are simulated.
32 devices in a mesh: tile: 8 (over z, core), tmpl: 4 (over y, x).
Axes of the slice: x: 2, y: 2, z: 4, core: 2. Of those that a mesh axis runs over, the one named last changes fastest.
Arguments:
- sky_image: float32 [10, 128, 2048], P(None, 'tile'), may hold values from -8 to 8
- inverse_var: float32 [10, 128, 2048], P(None, 'tile'), may hold values from 0.3 to 3
- kernel_taps: float32 [10, 17], replicated, may hold values from 0.2 to 1
- kernel_sizes: int32 [10], replicated, may hold values from 1 to 8, as said below
- templates: float32 [10, 2048], P(None, 'tmpl'), may hold values from 0.1 to 10
- grid_index: int32 [3, 2048], P(None, 'tmpl'), may hold values from 0 to 63
Outputs:
- post_means: float32 [3, 128, 2048], P(None, 'tile', 'tmpl')
- log_evidence: float32 [128, 2048], P('tile', 'tmpl')
Inputs may be any that keep to these rules, and one draw needn't show every extreme that they name: `kernel_sizes`: some band has half-width 8 and some other band has half-width 1.
All inputs are finite; a program needn't handle non-finite values.
Results may differ from a plain program's by a relative error of at most 0.0003.
Values sent between devices are 32-bit elements; how exact they have to be, the bound alone decides.
A program may use at most 64 MiB of HBM per device.

v0:
```python
import math

import jax
import jax.numpy as jnp
from jax import lax
from jax.sharding import PartitionSpec as P

GRID = 64


def with_halo(x, sides, width):
    for axis, dim in sides:
        count, length = (lax.axis_size(axis), x.shape[dim])
        up = [(i, (i + 1) % count) for i in range(count - 1)]
        down = [(j, i) for i, j in up]
        last = lax.slice_in_dim(x, length - width, length, axis=dim)
        leading = lax.slice_in_dim(x, 0, width, axis=dim)
        before = lax.ppermute(last, axis, up)
        after = lax.ppermute(leading, axis, down)
        x = jnp.concatenate([before, x, after], axis=dim)
    return x


def kernel_table(kernel_taps, kernel_sizes, radius):
    offsets = jnp.arange(2 * radius + 1, dtype=jnp.int32) - radius
    inside = jnp.abs(offsets)[None, :] <= kernel_sizes[:, None]
    masked = jnp.where(inside, kernel_taps, jnp.float32(0.0))
    return masked / jnp.sum(masked, axis=1, keepdims=True)


def convolve_rows(padded, kernel, height, radius):
    result = jnp.zeros((padded.shape[0], height, padded.shape[2]), jnp.float32)
    for offset in range(2 * radius + 1):
        result = result + kernel[:, offset, None, None] * padded[:, offset : offset + height, :]
    return result


def convolve_cols(padded, kernel, width, radius):
    result = jnp.zeros((padded.shape[0], padded.shape[1], width), jnp.float32)
    for offset in range(2 * radius + 1):
        result = result + kernel[:, offset, None, None] * padded[:, :, offset : offset + width]
    return result


def fit_pixels(flux, weight, bank, coords):
    bands, pixels = flux.shape
    block = math.gcd(pixels, 2048)
    count = pixels // block
    flux_blocks = flux.reshape(bands, count, block).transpose(1, 0, 2)
    weight_blocks = weight.reshape(bands, count, block).transpose(1, 0, 2)
    squared = bank * bank

    def one_block(pair):
        flux_part, weight_part = pair
        weighted = weight_part * flux_part
        self_term = jnp.sum(weighted * flux_part, axis=0)
        cross = jnp.einsum("bp,bk->pk", weighted, bank, precision=lax.Precision.HIGHEST)
        norm_tt = jnp.einsum("bp,bk->pk", weight_part, squared, precision=lax.Precision.HIGHEST)
        loglike = -0.5 * (self_term[:, None] - cross * cross / norm_tt)
        peak = jnp.max(loglike, axis=1)
        expo = jnp.exp(loglike - peak[:, None])
        total = jnp.sum(expo, axis=1)
        moments = jnp.einsum("pk,qk->qp", expo, coords, precision=lax.Precision.HIGHEST)
        return (peak, total, moments)

    peak, total, moments = lax.map(one_block, (flux_blocks, weight_blocks))
    return (
        peak.reshape(pixels),
        total.reshape(pixels),
        moments.transpose(1, 0, 2).reshape(3, pixels),
    )


def body(sky_image, inverse_var, kernel_taps, kernel_sizes, templates, grid_index):
    radius = (kernel_taps.shape[1] - 1) // 2
    bands, height, width = sky_image.shape
    shards = lax.axis_size("tmpl")
    col_block = width // shards
    col_start = lax.axis_index("tmpl") * col_block
    kernel = kernel_table(kernel_taps, kernel_sizes, radius)
    coords = (grid_index.astype(jnp.float32) + 0.5) / GRID
    padded_cols = jnp.pad(sky_image, ((0, 0), (0, 0), (radius, radius)))
    own_cols = lax.dynamic_slice_in_dim(padded_cols, col_start, col_block + 2 * radius, 2)
    extended = with_halo(own_cols, (("tile", 1),), radius)
    smooth = convolve_rows(extended, kernel, height, radius)
    flux = convolve_cols(smooth, kernel, col_block, radius)
    own_weight = lax.dynamic_slice_in_dim(inverse_var, col_start, col_block, 2)
    full_bank, full_coords = (
        lax.all_gather(templates, "tmpl", axis=1, tiled=True),
        lax.all_gather(coords, "tmpl", axis=1, tiled=True),
    )
    peak, total, moments = fit_pixels(
        flux.reshape(bands, height * col_block),
        own_weight.reshape(bands, height * col_block),
        full_bank,
        full_coords,
    )
    peak = peak.reshape(height, col_block)
    total = total.reshape(height, col_block)
    moments = moments.reshape(3, height, col_block)
    post_means = moments / total[None]
    log_evidence = peak + jnp.log(total)
    return (post_means, log_evidence)


def solution(mesh):
    placed = (
        P(None, "tile", None),
        P(None, "tile", None),
        P(),
        P(),
        P(None, "tmpl"),
        P(None, "tmpl"),
    )
    return jax.shard_map(
        body,
        mesh=mesh,
        in_specs=placed,
        out_specs=(P(None, "tile", "tmpl"), P("tile", "tmpl")),
        check_vma=False,
    )
```

profile of v0, /device:TPU:20, one launch (start us, length us, event | category | flops | bytes accessed | tf_op | source)
XLA Modules:
  0.0 271.7 jit_solution(15656260316578677356)
XLA Ops:
  0.6 0.0 copy-start
  0.6 1.3 pad_dynamic-slice_fusion.1
  2.0 1.9 collective-permute-start
  3.9 3.6 %collective-permute-start.1 = (f32[10,8,528]{2,1,0:T(8,128)S(1)}, f32[10,8,528]{2,1,0:T(8,128)S(1)}, u32[]{:S(2)}, u32[]{:S(2)}) collective-permute-start(f32[10,8,528]{2,1,0:T(8,128)S(1)} %get-tuple-element.103), channel_id=1, source_target_pairs={{4,0},{8,4},{12,8},{16,12},{20,16},{24,20},{28,24},{5,1},{9,5},{13... | collective-permute-start | bytes 506888 | tf_op jit(solution)/shard_map/ppermute | solution.py:19
  7.6 0.9 fusion.73
  8.4 0.8 fusion.72
  9.2 0.7 add_multiply_fusion
  9.9 0.0 copy-done
  10.0 0.5 slice_reduce_fusion.16
  10.4 0.2 reshape_reshape.13
  10.7 8.4 %all_gather.6 = f32[10,2048]{1,0:T(8,128)S(1)} all-gather(f32[10,512]{1,0:T(8,128)} %param.12), channel_id=1, replica_groups=mesh['tile'=8,'tmpl'=4] {'tmpl'}, dimensions={1}, use_global_device_ids=true | all-gather | bytes 102400 | tf_op jit(solution)/shard_map/all_gather | solution.py:89
  19.1 7.4 %all_gather.7 = f32[3,2048]{1,0:T(4,128)S(1)} all-gather(f32[3,512]{1,0:T(4,128)S(1)} %add_multiply_fusion), channel_id=1, replica_groups=mesh['tile'=8,'tmpl'=4] {'tmpl'}, dimensions={1}, use_global_device_ids=true | all-gather | bytes 30720 | tf_op jit(solution)/shard_map/all_gather | solution.py:90
  26.5 1.2 pad_dynamic-slice_fusion.2
  27.7 0.0 collective-permute-done
  27.7 0.0 collective-permute-done.1
  27.7 1.3 fusion.13
  29.1 1.8 fusion.56
  30.9 0.2 reshape_reshape.14
  31.1 239.2 %while.14 = (s32[]{:T(128)}, f32[4,2048]{1,0:T(4,128)S(1)}, f32[4,2048]{1,0:T(4,128)S(1)}, f32[4,3,2048]{2,1,0:T(4,128)S(1)}, f32[4,10,2048]{2,0,1:T(4,128)S(1)}...) while((s32[]{:T(128)}, f32[4,2048]{1,0:T(4,128)S(1)}, ...), condition=%wide.region_5.6_spmd, body=%wide.region_1.5_spmd.sunk | while | flops 1191258112 | bytes 152043664 | solution.py:66
  31.3 0.2 constant_dynamic-slice_fusion.4
  31.4 0.1 fusion.90
  31.5 15.9 %fusion.89 = f32[2048,2048]{0,1:T(8,128)} fusion(f32[10,2048]{1,0:T(8,128)S(1)} %get-tuple-element.196, f32[1,10,2048]{2,0,1:T(1,128)S(1)} %get-tuple-element.163), kind=kOutput, calls=%fused_computation.12.clone.1 | convolution fusion | flops 503316480 | bytes 16941056 | tf_op jit(solution)/shard_map/while/body/eval_jaxpr/bp,bk->pk/dot_general | solution.py:58
  47.4 19.2 %fusion.91 = (f32[2048]{0:T(1024)S(1)}, f32[2048,2048]{0,1:T(8,128)S(1)}) fusion(f32[2048,2048]{0,1:T(8,128)} %fusion.89, f32[10,2048]{1,0:T(8,128)S(1)} %get-tuple-element.195, f32[1,10,2048]{2,0,1:T(1,128)S(1)} %get-tuple-element.164, f32[1,10,2048]{2,0,1:T(1,128)S(1)} %get-tuple-element.163, f32[2048]{0:T(1024)S(1)} %fusion.90), kind=kOutput, calls=%fused_computation.152.clone.1 | convolution fusion | flops 524306432 | bytes 33816576 | tf_op jit(solution)/shard_map/while/body/eval_jaxpr/bp,bk->pk/dot_general | solution.py:57
  66.7 0.0 copy-start.1
  66.7 5.7 %copy-done.1 = f32[2048,2048]{0,1:T(8,128)} copy-done((f32[2048,2048]{0,1:T(8,128)}, f32[2048,2048]{0,1:T(8,128)S(1)}, u32[]{:S(2)}) %copy-start.1) | copy-done | bytes 16777240 | tf_op jit(solution)/shard_map/while
  72.4 10.3 %fusion.93 = f32[4,3,2048]{2,1,0:T(4,128)S(1)} fusion(f32[4,3,2048]{2,1,0:T(4,128)S(1)} %get-tuple-element.181, s32[]{:T(128)} %get-tuple-element.178, f32[3,2048]{1,0:T(4,128)S(1)} %get-tuple-element.197, f32[2048,2048]{0,1:T(8,128)S(1)} %get-tuple-element.166, f32[2048]{0:T(1024)S(1)} %get-tuple-element.165), kind=kOutput, calls=%fused_computation.6.clone.1 | convolution fusion | flops 155189248 | bytes 16850948 | tf_op jit(solution)/shard_map/while/body/eval_jaxpr/pk,qk->qp/dot_general | solution.py:63
  82.7 8.1 %fusion.92 = f32[2048]{0:T(1024)S(1)} fusion(f32[2048,2048]{0,1:T(8,128)} %copy-done.1, f32[2048]{0:T(1024)S(1)} %get-tuple-element.165), kind=kLoop, calls=%fused_computation.3.clone.1 | loop fusion | flops 8386560 | bytes 16793600 | tf_op jit(solution)/shard_map/while/body/eval_jaxpr/reduce_sum | solution.py:62
  90.7 0.1 dynamic_update_slice.17
  90.9 0.1 dynamic_update_slice.16
  91.0 0.2 constant_dynamic-slice_fusion.4
  91.2 0.1 fusion.90
  91.3 15.9 %fusion.89 = f32[2048,2048]{0,1:T(8,128)} fusion(f32[10,2048]{1,0:T(8,128)S(1)} %get-tuple-element.196, f32[1,10,2048]{2,0,1:T(1,128)S(1)} %get-tuple-element.163), kind=kOutput, calls=%fused_computation.12.clone.1 | convolution fusion | flops 503316480 | bytes 16941056 | tf_op jit(solution)/shard_map/while/body/eval_jaxpr/bp,bk->pk/dot_general | solution.py:58
  107.2 19.2 %fusion.91 = (f32[2048]{0:T(1024)S(1)}, f32[2048,2048]{0,1:T(8,128)S(1)}) fusion(f32[2048,2048]{0,1:T(8,128)} %fusion.89, f32[10,2048]{1,0:T(8,128)S(1)} %get-tuple-element.195, f32[1,10,2048]{2,0,1:T(1,128)S(1)} %get-tuple-element.164, f32[1,10,2048]{2,0,1:T(1,128)S(1)} %get-tuple-element.163, f32[2048]{0:T(1024)S(1)} %fusion.90), kind=kOutput, calls=%fused_computation.152.clone.1 | convolution fusion | flops 524306432 | bytes 33816576 | tf_op jit(solution)/shard_map/while/body/eval_jaxpr/bp,bk->pk/dot_general | solution.py:57
  126.4 0.0 copy-start.1
  126.4 5.7 %copy-done.1 = f32[2048,2048]{0,1:T(8,128)} copy-done((f32[2048,2048]{0,1:T(8,128)}, f32[2048,2048]{0,1:T(8,128)S(1)}, u32[]{:S(2)}) %copy-start.1) | copy-done | bytes 16777240 | tf_op jit(solution)/shard_map/while
  132.1 10.3 %fusion.93 = f32[4,3,2048]{2,1,0:T(4,128)S(1)} fusion(f32[4,3,2048]{2,1,0:T(4,128)S(1)} %get-tuple-element.181, s32[]{:T(128)} %get-tuple-element.178, f32[3,2048]{1,0:T(4,128)S(1)} %get-tuple-element.197, f32[2048,2048]{0,1:T(8,128)S(1)} %get-tuple-element.166, f32[2048]{0:T(1024)S(1)} %get-tuple-element.165), kind=kOutput, calls=%fused_computation.6.clone.1 | convolution fusion | flops 155189248 | bytes 16850948 | tf_op jit(solution)/shard_map/while/body/eval_jaxpr/pk,qk->qp/dot_general | solution.py:63
  142.4 8.1 %fusion.92 = f32[2048]{0:T(1024)S(1)} fusion(f32[2048,2048]{0,1:T(8,128)} %copy-done.1, f32[2048]{0:T(1024)S(1)} %get-tuple-element.165), kind=kLoop, calls=%fused_computation.3.clone.1 | loop fusion | flops 8386560 | bytes 16793600 | tf_op jit(solution)/shard_map/while/body/eval_jaxpr/reduce_sum | solution.py:62
  150.5 0.1 dynamic_update_slice.17
  150.6 0.1 dynamic_update_slice.16
  150.8 0.2 constant_dynamic-slice_fusion.4
  150.9 0.1 fusion.90
  151.0 15.9 %fusion.89 = f32[2048,2048]{0,1:T(8,128)} fusion(f32[10,2048]{1,0:T(8,128)S(1)} %get-tuple-element.196, f32[1,10,2048]{2,0,1:T(1,128)S(1)} %get-tuple-element.163), kind=kOutput, calls=%fused_computation.12.clone.1 | convolution fusion | flops 503316480 | bytes 16941056 | tf_op jit(solution)/shard_map/while/body/eval_jaxpr/bp,bk->pk/dot_general | solution.py:58
  166.9 19.2 %fusion.91 = (f32[2048]{0:T(1024)S(1)}, f32[2048,2048]{0,1:T(8,128)S(1)}) fusion(f32[2048,2048]{0,1:T(8,128)} %fusion.89, f32[10,2048]{1,0:T(8,128)S(1)} %get-tuple-element.195, f32[1,10,2048]{2,0,1:T(1,128)S(1)} %get-tuple-element.164, f32[1,10,2048]{2,0,1:T(1,128)S(1)} %get-tuple-element.163, f32[2048]{0:T(1024)S(1)} %fusion.90), kind=kOutput, calls=%fused_computation.152.clone.1 | convolution fusion | flops 524306432 | bytes 33816576 | tf_op jit(solution)/shard_map/while/body/eval_jaxpr/bp,bk->pk/dot_general | solution.py:57
  186.2 0.0 copy-start.1
  186.2 5.7 %copy-done.1 = f32[2048,2048]{0,1:T(8,128)} copy-done((f32[2048,2048]{0,1:T(8,128)}, f32[2048,2048]{0,1:T(8,128)S(1)}, u32[]{:S(2)}) %copy-start.1) | copy-done | bytes 16777240 | tf_op jit(solution)/shard_map/while
  191.9 10.3 %fusion.93 = f32[4,3,2048]{2,1,0:T(4,128)S(1)} fusion(f32[4,3,2048]{2,1,0:T(4,128)S(1)} %get-tuple-element.181, s32[]{:T(128)} %get-tuple-element.178, f32[3,2048]{1,0:T(4,128)S(1)} %get-tuple-element.197, f32[2048,2048]{0,1:T(8,128)S(1)} %get-tuple-element.166, f32[2048]{0:T(1024)S(1)} %get-tuple-element.165), kind=kOutput, calls=%fused_computation.6.clone.1 | convolution fusion | flops 155189248 | bytes 16850948 | tf_op jit(solution)/shard_map/while/body/eval_jaxpr/pk,qk->qp/dot_general | solution.py:63
  202.2 8.1 %fusion.92 = f32[2048]{0:T(1024)S(1)} fusion(f32[2048,2048]{0,1:T(8,128)} %copy-done.1, f32[2048]{0:T(1024)S(1)} %get-tuple-element.165), kind=kLoop, calls=%fused_computation.3.clone.1 | loop fusion | flops 8386560 | bytes 16793600 | tf_op jit(solution)/shard_map/while/body/eval_jaxpr/reduce_sum | solution.py:62
  210.2 0.1 dynamic_update_slice.17
  210.4 0.1 dynamic_update_slice.16
  210.5 0.2 constant_dynamic-slice_fusion.4
  210.7 0.1 fusion.90
  210.8 15.9 %fusion.89 = f32[2048,2048]{0,1:T(8,128)} fusion(f32[10,2048]{1,0:T(8,128)S(1)} %get-tuple-element.196, f32[1,10,2048]{2,0,1:T(1,128)S(1)} %get-tuple-element.163), kind=kOutput, calls=%fused_computation.12.clone.1 | convolution fusion | flops 503316480 | bytes 16941056 | tf_op jit(solution)/shard_map/while/body/eval_jaxpr/bp,bk->pk/dot_general | solution.py:58
  226.7 19.2 %fusion.91 = (f32[2048]{0:T(1024)S(1)}, f32[2048,2048]{0,1:T(8,128)S(1)}) fusion(f32[2048,2048]{0,1:T(8,128)} %fusion.89, f32[10,2048]{1,0:T(8,128)S(1)} %get-tuple-element.195, f32[1,10,2048]{2,0,1:T(1,128)S(1)} %get-tuple-element.164, f32[1,10,2048]{2,0,1:T(1,128)S(1)} %get-tuple-element.163, f32[2048]{0:T(1024)S(1)} %fusion.90), kind=kOutput, calls=%fused_computation.152.clone.1 | convolution fusion | flops 524306432 | bytes 33816576 | tf_op jit(solution)/shard_map/while/body/eval_jaxpr/bp,bk->pk/dot_general | solution.py:57
  245.9 0.0 copy-start.1
  245.9 5.7 %copy-done.1 = f32[2048,2048]{0,1:T(8,128)} copy-done((f32[2048,2048]{0,1:T(8,128)}, f32[2048,2048]{0,1:T(8,128)S(1)}, u32[]{:S(2)}) %copy-start.1) | copy-done | bytes 16777240 | tf_op jit(solution)/shard_map/while
  251.6 10.3 %fusion.93 = f32[4,3,2048]{2,1,0:T(4,128)S(1)} fusion(f32[4,3,2048]{2,1,0:T(4,128)S(1)} %get-tuple-element.181, s32[]{:T(128)} %get-tuple-element.178, f32[3,2048]{1,0:T(4,128)S(1)} %get-tuple-element.197, f32[2048,2048]{0,1:T(8,128)S(1)} %get-tuple-element.166, f32[2048]{0:T(1024)S(1)} %get-tuple-element.165), kind=kOutput, calls=%fused_computation.6.clone.1 | convolution fusion | flops 155189248 | bytes 16850948 | tf_op jit(solution)/shard_map/while/body/eval_jaxpr/pk,qk->qp/dot_general | solution.py:63
  261.9 8.1 %fusion.92 = f32[2048]{0:T(1024)S(1)} fusion(f32[2048,2048]{0,1:T(8,128)} %copy-done.1, f32[2048]{0:T(1024)S(1)} %get-tuple-element.165), kind=kLoop, calls=%fused_computation.3.clone.1 | loop fusion | flops 8386560 | bytes 16793600 | tf_op jit(solution)/shard_map/while/body/eval_jaxpr/reduce_sum | solution.py:62
  270.0 0.1 dynamic_update_slice.17
  270.1 0.1 dynamic_update_slice.16
  270.3 0.1 copy.11
  270.4 0.1 reshape_reshape.15
  270.4 0.6 log_add_fusion
  271.1 0.7 broadcast_divide_fusion
  (8 shorter events, 0.1 us)
Async XLA Ops:
  0.6 9.3 %copy-start = (f32[10,16,2048]{2,1,0:T(8,128)S(1)}, f32[10,16,2048]{2,1,0:T(8,128)}, u32[]{:S(2)}) copy-start(f32[10,16,2048]{2,1,0:T(8,128)} %param.9) | copy-start | bytes 3932164
  2.0 25.7 %collective-permute-start = (f32[10,8,528]{2,1,0:T(8,128)S(1)}, f32[10,8,528]{2,1,0:T(8,128)S(1)}, u32[]{:S(2)}, u32[]{:S(2)}) collective-permute-start(f32[10,8,528]{2,1,0:T(8,128)S(1)} %get-tuple-element.102), channel_id=1, source_target_pairs={{0,4},{4,8},{8,12},{12,16},{16,20},{20,24},{24,28},{1,5},{5,9},{9,... | collective-permute-start | bytes 506888 | tf_op jit(solution)/shard_map/ppermute | solution.py:18
  3.9 23.8 %collective-permute-start.1 = (f32[10,8,528]{2,1,0:T(8,128)S(1)}, f32[10,8,528]{2,1,0:T(8,128)S(1)}, u32[]{:S(2)}, u32[]{:S(2)}) collective-permute-start(f32[10,8,528]{2,1,0:T(8,128)S(1)} %get-tuple-element.103), channel_id=1, source_target_pairs={{4,0},{8,4},{12,8},{16,12},{20,16},{24,20},{28,24},{5,1},{9,5},{13... | collective-permute-start | bytes 506888 | tf_op jit(solution)/shard_map/ppermute | solution.py:19
  66.7 5.7 %copy-start.1 = (f32[2048,2048]{0,1:T(8,128)}, f32[2048,2048]{0,1:T(8,128)S(1)}, u32[]{:S(2)}) copy-start(f32[2048,2048]{0,1:T(8,128)S(1)} %get-tuple-element.166) | copy-start | bytes 50331652 | tf_op jit(solution)/shard_map/while
  126.4 5.7 %copy-start.1 = (f32[2048,2048]{0,1:T(8,128)}, f32[2048,2048]{0,1:T(8,128)S(1)}, u32[]{:S(2)}) copy-start(f32[2048,2048]{0,1:T(8,128)S(1)} %get-tuple-element.166) | copy-start | bytes 50331652 | tf_op jit(solution)/shard_map/while
  186.2 5.7 %copy-start.1 = (f32[2048,2048]{0,1:T(8,128)}, f32[2048,2048]{0,1:T(8,128)S(1)}, u32[]{:S(2)}) copy-start(f32[2048,2048]{0,1:T(8,128)S(1)} %get-tuple-element.166) | copy-start | bytes 50331652 | tf_op jit(solution)/shard_map/while
  245.9 5.7 %copy-start.1 = (f32[2048,2048]{0,1:T(8,128)}, f32[2048,2048]{0,1:T(8,128)S(1)}, u32[]{:S(2)}) copy-start(f32[2048,2048]{0,1:T(8,128)S(1)} %get-tuple-element.166) | copy-start | bytes 50331652 | tf_op jit(solution)/shard_map/while
where the time goes:
time: 273 us; the launch traced here: 272 us
  matrix products  182 us (67%)
  other arithmetic  39.4 us (14%)
  local copies, waits for them, and re-layouts  28.1 us (10%)
  blocking collectives  15.8 us (6%)
  starting transfers between devices  5.56 us (2%)
    dot_general x4, matrix products, one_block(): jnp.einsum('bp,bk->pk', weighted, bank, precision=lax.Precision.HIGHEST)  77 us
    dot_general x4, matrix products, one_block(): jnp.einsum('bp,bk->pk', weight_part, squared, precision=lax.Precision.HIG...  63.6 us
    dot_general x4, matrix products, one_block(): jnp.einsum('pk,qk->qp', expo, coords, precision=lax.Precision.HIGHEST)  41.1 us
    reduce_sum x4, other arithmetic, one_block(): total = jnp.sum(expo, axis=1)  32.3 us
    while x8, local copies, waits for them, and re-layouts  22.8 us
    all_gather x1, blocking collectives, body(): lax.all_gather(templates, 'tmpl', axis=1, tiled=True)  8.43 us
    all_gather x1, blocking collectives, body(): lax.all_gather(coords, 'tmpl', axis=1, tiled=True)  7.38 us
  transfers between devices with their start and end apart: 2, of which 0 were waited for; matrix products, arithmetic and copies ran while one was open for 2% of the time, Pallas kernels for 0%

commit v1 on v0

v1 whole, which is shorter than its diff:
```python
import math

import jax
import jax.numpy as jnp
from jax import lax
from jax.experimental import pallas as pl
from jax.experimental.pallas import tpu as pltpu
from jax.sharding import PartitionSpec as P

GRID = 64
PIECE = 16
SCALE = math.sqrt(0.5 * math.log2(math.e))
SAFE = 100.0


def with_halo(x, sides, width):
    for axis, dim in sides:
        count, length = (lax.axis_size(axis), x.shape[dim])
        up = [(i, (i + 1) % count) for i in range(count - 1)]
        down = [(j, i) for i, j in up]
        last = lax.slice_in_dim(x, length - width, length, axis=dim)
        leading = lax.slice_in_dim(x, 0, width, axis=dim)
        before = lax.ppermute(last, axis, up)
        after = lax.ppermute(leading, axis, down)
        x = jnp.concatenate([before, x, after], axis=dim)
    return x


def kernel_table(kernel_taps, kernel_sizes, radius):
    offsets = jnp.arange(2 * radius + 1, dtype=jnp.int32) - radius
    inside = jnp.abs(offsets)[None, :] <= kernel_sizes[:, None]
    masked = jnp.where(inside, kernel_taps, jnp.float32(0.0))
    return masked / jnp.sum(masked, axis=1, keepdims=True)


def convolve_rows(padded, kernel, height, radius):
    result = jnp.zeros((padded.shape[0], height, padded.shape[2]), jnp.float32)
    for offset in range(2 * radius + 1):
        result = result + kernel[:, offset, None, None] * padded[:, offset : offset + height, :]
    return result


def convolve_cols(padded, kernel, width, radius):
    result = jnp.zeros((padded.shape[0], padded.shape[1], width), jnp.float32)
    for offset in range(2 * radius + 1):
        result = result + kernel[:, offset, None, None] * padded[:, :, offset : offset + width]
    return result


def split3(x):
    high = x.astype(jnp.bfloat16).astype(jnp.float32)
    rest = x - high
    mid = rest.astype(jnp.bfloat16).astype(jnp.float32)
    low = (rest - mid).astype(jnp.bfloat16).astype(jnp.float32)
    return high, mid, low


def left_terms(x):
    h, m, l = split3(x)
    return jnp.concatenate([h, h, h, m, m, l, m, l], axis=0)


def right_terms(x):
    h, m, l = split3(x)
    return jnp.concatenate([h, m, l, h, m, h, l, m], axis=0)


def dot(a, b):
    return lax.dot_general(a, b, (((1,), (0,)), ((), ())), preferred_element_type=jnp.float32)


def fit_kernel(chunk, bank_ref, coords_ref, flux_ref, weight_ref, out_ref, lin, sqr, crd):
    ntmpl = bank_ref.shape[1]

    @pl.when(pl.program_id(0) == 0)
    def _():
        bank = bank_ref[...]
        lin[...] = right_terms(bank).T.astype(jnp.bfloat16)
        sqr[...] = right_terms(bank * bank).T.astype(jnp.bfloat16)
        crd[...] = coords_ref[...].astype(jnp.bfloat16)

    flux, weight = flux_ref[...], weight_ref[...]
    weighted = weight * flux
    half = 0.5 * jnp.sum(weighted * flux, axis=0, keepdims=True)
    cross_rhs = left_terms(weighted * SCALE).astype(jnp.bfloat16)
    norm_rhs = left_terms(weight).astype(jnp.bfloat16)

    def gain(rows):
        cross = dot(lin[rows, :], cross_rhs)
        norm = dot(sqr[rows, :], norm_rhs)
        return cross * cross * pl.reciprocal(norm, approx=True)

    def sums(rows, expo):
        high = expo.astype(jnp.bfloat16)
        low = (expo - high.astype(jnp.float32)).astype(jnp.bfloat16)
        return dot(crd[:, rows], high) + dot(crd[:, rows], low)

    def finish(acc, shift):
        total = acc[3:4]
        out_ref[0:3, :] = acc[0:3] / total
        out_ref[3:4, :] = (shift * math.log(2.0) - half) + jnp.log(total)

    small = jnp.max(half) <= SAFE * math.log(2.0)

    @pl.when(small)
    def _():
        acc = jnp.zeros((PIECE, flux.shape[1]), jnp.float32)
        for start in range(0, ntmpl, chunk):
            rows = pl.ds(start, chunk)
            acc = acc + sums(rows, jnp.exp2(gain(rows)))
        finish(acc, jnp.zeros_like(half))

    @pl.when(jnp.logical_not(small))
    def _():
        def step(i, carry):
            acc, peak = carry
            rows = pl.ds(pl.multiple_of(i * chunk, chunk), chunk)
            values = gain(rows)
            later = jnp.maximum(peak, jnp.max(values, axis=0, keepdims=True))
            return acc * jnp.exp2(peak - later) + sums(rows, jnp.exp2(values - later)), later

        acc, peak = lax.fori_loop(
            0,
            ntmpl // chunk,
            step,
            (jnp.zeros((PIECE, flux.shape[1]), jnp.float32), jnp.zeros_like(half)),
        )
        finish(acc, peak)


def fit_pixels(flux, weight, bank, coords):
    pixels, ntmpl = flux.shape[1], bank.shape[1]
    block = math.gcd(pixels, 256)
    chunk = math.gcd(ntmpl, 256)
    out = pl.pallas_call(
        lambda *refs: fit_kernel(chunk, *refs),
        grid=(pixels // block,),
        in_specs=[
            pl.BlockSpec((PIECE, ntmpl), lambda i: (0, 0)),
            pl.BlockSpec((PIECE, ntmpl), lambda i: (0, 0)),
            pl.BlockSpec((PIECE, block), lambda i: (0, i)),
            pl.BlockSpec((PIECE, block), lambda i: (0, i)),
        ],
        out_specs=pl.BlockSpec((4, block), lambda i: (0, i)),
        out_shape=jax.ShapeDtypeStruct((4, pixels), jnp.float32),
        scratch_shapes=[
            pltpu.VMEM((ntmpl, 8 * PIECE), jnp.bfloat16),
            pltpu.VMEM((ntmpl, 8 * PIECE), jnp.bfloat16),
            pltpu.VMEM((PIECE, ntmpl), jnp.bfloat16),
        ],
        compiler_params=pltpu.CompilerParams(vmem_limit_bytes=40 * 2**20),
    )(bank, coords, flux, weight)
    return out


def pad_bands(x):
    return jnp.pad(x, ((0, PIECE - x.shape[0]),) + ((0, 0),) * (x.ndim - 1))


def body(sky_image, inverse_var, kernel_taps, kernel_sizes, templates, grid_index):
    radius = (kernel_taps.shape[1] - 1) // 2
    bands, height, width = sky_image.shape
    shards = lax.axis_size("tmpl")
    col_block = width // shards
    col_start = lax.axis_index("tmpl") * col_block
    kernel = kernel_table(kernel_taps, kernel_sizes, radius)
    coords = (grid_index.astype(jnp.float32) + 0.5) / GRID
    table = lax.all_gather(jnp.concatenate([templates, coords], axis=0), "tmpl", axis=1, tiled=True)
    padded_cols = jnp.pad(sky_image, ((0, 0), (0, 0), (radius, radius)))
    own_cols = lax.dynamic_slice_in_dim(padded_cols, col_start, col_block + 2 * radius, 2)
    extended = with_halo(own_cols, (("tile", 1),), radius)
    smooth = convolve_rows(extended, kernel, height, radius)
    flux = convolve_cols(smooth, kernel, col_block, radius)
    own_weight = lax.dynamic_slice_in_dim(inverse_var, col_start, col_block, 2)
    full_coords = jnp.concatenate([table[bands:], jnp.ones_like(table[:1])], axis=0)
    out = fit_pixels(
        pad_bands(flux.reshape(bands, height * col_block)),
        pad_bands(own_weight.reshape(bands, height * col_block)),
        pad_bands(table[:bands]),
        pad_bands(full_coords),
    )
    out = out.reshape(4, height, col_block)
    return out[:3], out[3]


def solution(mesh):
    placed = (
        P(None, "tile", None),
        P(None, "tile", None),
        P(),
        P(),
        P(None, "tmpl"),
        P(None, "tmpl"),
    )
    return jax.shard_map(
        body,
        mesh=mesh,
        in_specs=placed,
        out_specs=(P(None, "tile", "tmpl"), P("tile", "tmpl")),
        check_vma=False,
    )
```

time: 273 us -> 134 us (0.49)
  matrix products: 182 us -> 0 us
  Pallas kernels: 0 us -> 110 us
  other arithmetic: 39.4 us -> 3.4 us
  local copies, waits for them, and re-layouts: 28.1 us -> 5.12 us
  blocking collectives: 15.8 us -> 8.43 us
    dot_general x12 -> x0, matrix products: 182 us -> none  [the longest x4 77 us: one_block(): jnp.einsum('bp,bk->pk', weighted, bank, precision=lax.Precision.HIGHEST)]
    pallas_call x0 -> x1, Pallas kernels: none -> 110 us  [fit_pixels(): pl.pallas_call(lambda *refs: fit_kernel(chunk, *refs), grid=(pixels // bl...]
    reduce_sum x8 -> x0, other arithmetic: 32.6 us -> none  [the longest x4 32.3 us: one_block(): total = jnp.sum(expo, axis=1)]
    while x8 -> x0, local copies, waits for them, and re-layouts: 22.8 us -> none
    all_gather x2 -> x1, blocking collectives: 15.8 us -> 8.43 us  [body(): lax.all_gather(jnp.concatenate([templates, coords], axis=0), 'tmpl', axis...]
  transfers between devices with their start and end apart: 2 -> 2, of which waited for: 0 -> 0; matrix products, arithmetic and copies ran while one was open for 2% -> 1% of each run, Pallas kernels for 0% -> 0%
where the time goes in v1:
time: 134 us; the launch traced here: 133 us
  Pallas kernels  110 us (82%)
  blocking collectives  8.43 us (6%)
  starting transfers between devices  5.56 us (4%)
  local copies, waits for them, and re-layouts  5.12 us (4%)
  other arithmetic  3.4 us (3%)
    pallas_call x1, Pallas kernels, fit_pixels(): pl.pallas_call(lambda *refs: fit_kernel(chunk, *refs), grid=(pixels // bl...  110 us
    all_gather x1, blocking collectives, body(): lax.all_gather(jnp.concatenate([templates, coords], axis=0), 'tmpl', axis...  8.43 us
    ppermute x1, starting transfers between devices, with_halo(): after = lax.ppermute(leading, axis, down)  3.64 us
  transfers between devices with their start and end apart: 2, of which 0 were waited for; matrix products, arithmetic and copies ran while one was open for 1% of the time, Pallas kernels for 0%

profile of v1, /device:TPU:20, one launch (start us, length us, event | category | flops | bytes accessed | tf_op | source)
XLA Modules:
  0.0 133.3 jit_solution(15840007216399470360)
XLA Ops:
  0.6 0.0 copy-start
  0.6 0.0 copy-start.3
  0.7 0.0 copy-start.5
  0.7 0.0 copy-start.4
  0.7 0.0 copy-start.2
  0.7 1.3 pad_dynamic-slice_fusion.1
  2.0 1.9 %collective-permute-start = (f32[10,8,528]{2,1,0:T(8,128)S(1)}, f32[10,8,528]{2,1,0:T(8,128)S(1)}, u32[]{:S(2)}, u32[]{:S(2)}) collective-permute-start(f32[10,8,528]{2,1,0:T(8,128)S(1)} %get-tuple-element.19), channel_id=1, source_target_pairs={{0,4},{4,8},{8,12},{12,16},{16,20},{20,24},{24,28},{1,5},{5,9},{9,... | collective-permute-start | bytes 506888 | tf_op jit(solution)/shard_map/ppermute | solution.py:23
  3.9 3.6 %collective-permute-start.1 = (f32[10,8,528]{2,1,0:T(8,128)S(1)}, f32[10,8,528]{2,1,0:T(8,128)S(1)}, u32[]{:S(2)}, u32[]{:S(2)}) collective-permute-start(f32[10,8,528]{2,1,0:T(8,128)S(1)} %get-tuple-element.20), channel_id=1, source_target_pairs={{4,0},{8,4},{12,8},{16,12},{20,16},{24,20},{28,24},{5,1},{9,5},{13... | collective-permute-start | bytes 506888 | tf_op jit(solution)/shard_map/ppermute | solution.py:24
  7.6 0.0 copy-done.3
  7.6 0.0 copy-done.5
  7.6 0.2 fusion.63
  7.8 0.1 fusion.62
  7.9 0.0 copy-done.4
  7.9 0.0 copy-done.2
  7.9 8.4 %all_gather.3 = f32[13,2048]{1,0:T(8,128)S(1)} all-gather(f32[13,512]{1,0:T(8,128)S(1)} %pad_maximum_fusion.2), channel_id=1, replica_groups=mesh['tile'=8,'tmpl'=4] {'tmpl'}, dimensions={1}, use_global_device_ids=true | all-gather | bytes 133120 | tf_op jit(solution)/shard_map/all_gather | solution.py:168
  16.4 0.0 copy-done
  16.4 0.5 slice_reduce_fusion.17
  17.0 0.0 copy-start.1
  17.0 0.3 copy.9
  17.4 0.9 copy-done.1
  18.3 0.2 pad_dynamic-slice_fusion.2
  18.5 0.0 collective-permute-done
  18.5 0.0 collective-permute-done.1
  18.5 1.3 %fusion.3 = f32[10,16,528]{2,1,0:T(8,128)S(1)} fusion(f32[10,16,528]{2,1,0:T(8,128)S(1)} %pad_dynamic-slice_fusion.2, f32[10,8,528]{2,1,0:T(8,128)S(1)} %collective-permute-done.1, f32[10,8,528]{2,1,0:T(8,128)S(1)} %collective-permute-done, f32[10]{0:T(128)S(1)} %get-tuple-element.3, f32[10]{0:T(128)S(1)} %get-tuple-element.4, f32[10]{0:T(128)S(1)} %get-tuple-element.5, ...), kind=kLoop, calls=%fused_computation.34 | loop fusion | flops 4139520 | bytes 1014440 | tf_op jit(solution)/shard_map/add | solution.py:39
  19.8 1.8 %fusion.46 = f32[10,16,512]{2,1,0:T(8,128)S(1)} fusion(f32[10,16,528]{2,1,0:T(8,128)S(1)} %fusion.3, f32[10]{0:T(128)S(1)} %get-tuple-element.3, f32[10]{0:T(128)S(1)} %get-tuple-element.4, f32[10]{0:T(128)S(1)} %get-tuple-element.5, f32[10]{0:T(128)S(1)} %get-tuple-element.6, f32[10]{0:T(128)S(1)} %get-tuple-element.7, f32[10]{0:T(128)S(1)} %get-tuple-element.8, ...), kind=kLoop, calls=%fused_computation.80 | loop fusion | flops 2703360 | bytes 5898920 | tf_op jit(solution)/shard_map/add | solution.py:46
  21.7 0.3 copy.8
  22.0 109.8 %shard_map.77 = f32[4,8192]{1,0:T(4,128)S(1)} custom-call(f32[16,2048]{1,0:T(8,128)S(1)} %pad.20.refs_0_, f32[16,2048]{1,0:T(8,128)S(1)} %pad_select_fusion.refs_1_, f32[16,8192]{1,0:T(8,128)S(1)} %pad.23.refs_2_, f32[16,8192]{1,0:T(8,128)S(1)} %pad.24.refs_3_), custom_call_target="tpu_custom_call" | custom-call | tf_op jit(solution)/shard_map/pallas_call | solution.py:135
  131.9 0.1 slice_reduce_fusion
  132.0 0.7 copy.12
  132.6 0.6 squeeze.3
  (11 shorter events, 0.3 us)
Async XLA Ops:
  0.6 15.8 %copy-start = (f32[10,16,2048]{2,1,0:T(8,128)S(1)}, f32[10,16,2048]{2,1,0:T(8,128)}, u32[]{:S(2)}) copy-start(f32[10,16,2048]{2,1,0:T(8,128)} %param.7) | copy-start | bytes 3932164
  0.6 7.0 %copy-start.3 = (f32[10,17]{1,0:T(8,128)S(1)}, f32[10,17]{1,0:T(8,128)}, u32[]{:S(2)}) copy-start(f32[10,17]{1,0:T(8,128)} %param.8) | copy-start | bytes 2044
  0.7 7.0 %copy-start.5 = (s32[10]{0:T(128)S(1)}, s32[10]{0:T(128)}, u32[]{:S(2)}) copy-start(s32[10]{0:T(128)} %param.9) | copy-start | bytes 124
  0.7 7.2 %copy-start.4 = (s32[3,512]{1,0:T(4,128)S(1)}, s32[3,512]{1,0:T(4,128)}, u32[]{:S(2)}) copy-start(s32[3,512]{1,0:T(4,128)} %param.11) | copy-start | bytes 18436
  0.7 7.2 %copy-start.2 = (f32[10,512]{1,0:T(8,128)S(1)}, f32[10,512]{1,0:T(8,128)}, u32[]{:S(2)}) copy-start(f32[10,512]{1,0:T(8,128)} %param.10) | copy-start | bytes 61444
  2.0 16.5 %collective-permute-start = (f32[10,8,528]{2,1,0:T(8,128)S(1)}, f32[10,8,528]{2,1,0:T(8,128)S(1)}, u32[]{:S(2)}, u32[]{:S(2)}) collective-permute-start(f32[10,8,528]{2,1,0:T(8,128)S(1)} %get-tuple-element.19), channel_id=1, source_target_pairs={{0,4},{4,8},{8,12},{12,16},{16,20},{20,24},{24,28},{1,5},{5,9},{9,... | collective-permute-start | bytes 506888 | tf_op jit(solution)/shard_map/ppermute | solution.py:23
  3.9 14.5 %collective-permute-start.1 = (f32[10,8,528]{2,1,0:T(8,128)S(1)}, f32[10,8,528]{2,1,0:T(8,128)S(1)}, u32[]{:S(2)}, u32[]{:S(2)}) collective-permute-start(f32[10,8,528]{2,1,0:T(8,128)S(1)} %get-tuple-element.20), channel_id=1, source_target_pairs={{4,0},{8,4},{12,8},{16,12},{20,16},{24,20},{28,24},{5,1},{9,5},{13... | collective-permute-start | bytes 506888 | tf_op jit(solution)/shard_map/ppermute | solution.py:24
  17.0 1.3 copy-start.1

commit v2 on v0

v2 whole, which is shorter than its diff:
```python
import math

import jax
import jax.numpy as jnp
from jax import lax
from jax.experimental import pallas as pl
from jax.experimental.pallas import tpu as pltpu
from jax.sharding import PartitionSpec as P

GRID = 64
PIECE = 16
SCALE = math.sqrt(0.5 * math.log2(math.e))
SAFE = 100.0


MESH = pl.DeviceIdType.MESH


def kernel_table(kernel_taps, kernel_sizes, radius):
    offsets = jnp.arange(2 * radius + 1, dtype=jnp.int32) - radius
    inside = jnp.abs(offsets)[None, :] <= kernel_sizes[:, None]
    masked = jnp.where(inside, kernel_taps, jnp.float32(0.0))
    return masked / jnp.sum(masked, axis=1, keepdims=True)


def prep_kernel(
    taps, sky, inverse_var, templates, grid_index,
    flux_out, weight_out, bank, index,
    win, weight, left, right, smooth,
    local_sem, side_sem, send_sem, recv_sem, bank_send, bank_recv,
):
    bands, height, _ = sky.shape
    radius = (taps.shape[1] - 1) // 2
    tile, tiles = lax.axis_index("tile"), lax.axis_size("tile")
    me, shards = lax.axis_index("tmpl"), lax.axis_size("tmpl")
    cols, edge = weight.shape[2], left.shape[2]
    held = templates.shape[1]
    own = pl.ds(pl.multiple_of(me * cols, 128), cols)
    inner = pl.ds(radius, height)

    center = pltpu.make_async_copy(sky.at[:, :, own], win.at[:, inner, pl.ds(0, cols)], local_sem.at[0])
    weights = pltpu.make_async_copy(inverse_var.at[:, :, own], weight, local_sem.at[1])
    before = pltpu.make_async_copy(
        sky.at[:, :, pl.ds(pl.multiple_of(lax.max(me * cols - edge, 0), 128), edge)], left, side_sem.at[0]
    )
    after = pltpu.make_async_copy(
        sky.at[:, :, pl.ds(pl.multiple_of(lax.min((me + 1) * cols, shards * cols - edge), 128), edge)],
        right,
        side_sem.at[1],
    )
    center.start()
    before.start()
    after.start()
    weights.start()

    barrier = pltpu.get_barrier_semaphore()
    peers = [lax.rem(me + s, shards) for s in range(1, shards)]
    for peer in peers:
        pl.semaphore_signal(barrier, inc=1, device_id={"tmpl": peer}, device_id_type=MESH)

    @pl.when(tile > 0)
    def _():
        pl.semaphore_signal(barrier, inc=1, device_id={"tile": tile - 1}, device_id_type=MESH)

    @pl.when(tile < tiles - 1)
    def _():
        pl.semaphore_signal(barrier, inc=1, device_id={"tile": tile + 1}, device_id_type=MESH)

    zero_rows = jnp.zeros((bands, radius, cols + edge), jnp.float32)

    center.wait()
    before.wait()
    after.wait()
    lane = lax.broadcasted_iota(jnp.int32, (bands, height, edge), 2)
    follows = jnp.where(me < shards - 1, right[...], 0.0)
    precedes = jnp.where(me > 0, left[...], 0.0)
    win[:, inner, pl.ds(cols, edge)] = jnp.where(lane < edge // 2, follows, precedes)

    neighbours = lax.min(tile, 1) + lax.min(tiles - 1 - tile, 1)
    pl.semaphore_wait(barrier, shards - 1 + neighbours)

    down = pltpu.make_async_remote_copy(
        src_ref=win.at[:, pl.ds(height, radius), :],
        dst_ref=win.at[:, pl.ds(0, radius), :],
        send_sem=send_sem.at[0],
        recv_sem=recv_sem.at[0],
        device_id={"tile": lax.min(tile + 1, tiles - 1)},
        device_id_type=MESH,
    )
    up = pltpu.make_async_remote_copy(
        src_ref=win.at[:, pl.ds(radius, radius), :],
        dst_ref=win.at[:, pl.ds(height + radius, radius), :],
        send_sem=send_sem.at[1],
        recv_sem=recv_sem.at[1],
        device_id={"tile": lax.max(tile - 1, 0)},
        device_id_type=MESH,
    )

    @pl.when(tile < tiles - 1)
    def _():
        down.start()

    @pl.when(tile > 0)
    def _():
        up.start()

    mine = pl.ds(pl.multiple_of(me * held, 128), held)
    copies = []
    for s, peer in enumerate(peers):
        for which, (source, target) in enumerate(((templates, bank), (grid_index, index))):
            copy = pltpu.make_async_remote_copy(
                src_ref=source,
                dst_ref=target.at[:, mine],
                send_sem=bank_send.at[which, s],
                recv_sem=bank_recv.at[which, s],
                device_id={"tmpl": peer},
                device_id_type=MESH,
            )
            copy.start()
            copies.append(copy)
    bank[:, mine] = templates[...]
    index[:, mine] = grid_index[...]

    def along_cols(band, rows):
        part = win[band, rows, :]
        total = taps[band, radius] * part[:, :cols]
        for t in range(2 * radius + 1):
            if t != radius:
                moved = pltpu.roll(part, (radius - t) % (cols + edge), 1)
                total = total + taps[band, t] * moved[:, :cols]
        smooth[band, rows, :] = total

    def own_rows(band, _):
        along_cols(band, inner)
        return 0

    lax.fori_loop(0, bands, own_rows, 0)
    weights.wait()
    pad = flux_out.shape[1] - bands
    if pad:
        blank = jnp.zeros((height, pad, cols), jnp.float32)
        flux_out[:, pl.ds(bands, pad), :] = blank
        weight_out[:, pl.ds(bands, pad), :] = blank
    for band in range(bands):
        weight_out[:, band, :] = weight[band]

    @pl.when(tile > 0)
    def _():
        down.wait_recv()

    @pl.when(tile == 0)
    def _():
        win[:, pl.ds(0, radius), :] = zero_rows

    @pl.when(tile < tiles - 1)
    def _():
        up.wait_recv()

    @pl.when(tile == tiles - 1)
    def _():
        win[:, pl.ds(height + radius, radius), :] = zero_rows

    def halo_rows(band, _):
        along_cols(band, pl.ds(0, radius))
        along_cols(band, pl.ds(height + radius, radius))
        return 0

    lax.fori_loop(0, bands, halo_rows, 0)
    for band in range(bands):
        total = taps[band, 0] * smooth[band, pl.ds(0, height), :]
        for t in range(1, 2 * radius + 1):
            total = total + taps[band, t] * smooth[band, pl.ds(t, height), :]
        flux_out[:, band, :] = total

    @pl.when(tile < tiles - 1)
    def _():
        down.wait_send()

    @pl.when(tile > 0)
    def _():
        up.wait_send()

    for copy in copies:
        copy.wait()


def prepare(taps, sky, inverse_var, templates, grid_index):
    bands, height, width = sky.shape
    radius = (taps.shape[1] - 1) // 2
    shards = lax.axis_size("tmpl")
    cols, edge = width // shards, 128
    ntmpl = templates.shape[1] * shards
    vmem = pl.BlockSpec(memory_space=pltpu.VMEM)
    anywhere = pl.BlockSpec(memory_space=pl.ANY)
    rows = height + 2 * radius
    return pl.pallas_call(
        prep_kernel,
        in_specs=[pl.BlockSpec(memory_space=pltpu.SMEM), anywhere, anywhere, vmem, vmem],
        out_specs=[vmem] * 4,
        out_shape=[
            jax.ShapeDtypeStruct((height, PIECE, cols), jnp.float32),
            jax.ShapeDtypeStruct((height, PIECE, cols), jnp.float32),
            jax.ShapeDtypeStruct((bands, ntmpl), jnp.float32),
            jax.ShapeDtypeStruct((grid_index.shape[0], ntmpl), jnp.int32),
        ],
        scratch_shapes=[
            pltpu.VMEM((bands, rows, cols + edge), jnp.float32),
            pltpu.VMEM((bands, height, cols), jnp.float32),
            pltpu.VMEM((bands, height, edge), jnp.float32),
            pltpu.VMEM((bands, height, edge), jnp.float32),
            pltpu.VMEM((bands, rows, cols), jnp.float32),
            pltpu.SemaphoreType.DMA((2,)),
            pltpu.SemaphoreType.DMA((2,)),
            pltpu.SemaphoreType.DMA((2,)),
            pltpu.SemaphoreType.DMA((2,)),
            pltpu.SemaphoreType.DMA((2, max(shards - 1, 1))),
            pltpu.SemaphoreType.DMA((2, max(shards - 1, 1))),
        ],
        compiler_params=pltpu.CompilerParams(
            collective_id=0, has_side_effects=True, vmem_limit_bytes=32 * 2**20
        ),
    )(taps, sky, inverse_var, templates, grid_index)


def split3(x):
    high = x.astype(jnp.bfloat16).astype(jnp.float32)
    rest = x - high
    mid = rest.astype(jnp.bfloat16).astype(jnp.float32)
    low = (rest - mid).astype(jnp.bfloat16).astype(jnp.float32)
    return high, mid, low


def left_terms(x):
    h, m, l = split3(x)
    return jnp.concatenate([h, h, h, m, m, l, m, l], axis=0)


def right_terms(x):
    h, m, l = split3(x)
    return jnp.concatenate([h, m, l, h, m, h, l, m], axis=0)


def dot(a, b):
    return lax.dot_general(a, b, (((1,), (0,)), ((), ())), preferred_element_type=jnp.float32)


def fit_kernel(block, chunk, bank_ref, index_ref, flux_ref, weight_ref, means_ref, evidence_ref, lin, sqr, crd):
    bands, ntmpl = bank_ref.shape
    height, _, cols = flux_ref.shape
    bank = jnp.concatenate([bank_ref[...], jnp.zeros((PIECE - bands, ntmpl), jnp.float32)], axis=0)
    lin[...] = right_terms(bank).T.astype(jnp.bfloat16)
    sqr[...] = right_terms(bank * bank).T.astype(jnp.bfloat16)
    coords = (index_ref[...].astype(jnp.float32) + 0.5) / GRID
    coords = jnp.concatenate([coords, jnp.zeros((8 - coords.shape[0], ntmpl), jnp.float32)], axis=0).T
    for i in range(3):
        crd[i] = jnp.broadcast_to(coords[:, i : i + 1], (ntmpl, 128))

    def folded(x):
        return jnp.sum(x.reshape(x.shape[0] // 8, 8, x.shape[1]), axis=0)

    def one_block(step, _):
        row = step // (cols // block)
        lanes = pl.ds(pl.multiple_of(lax.rem(step, cols // block) * block, block), block)
        flux, weight = flux_ref[row, :, lanes], weight_ref[row, :, lanes]
        weighted = weight * flux
        half = 0.5 * jnp.sum(weighted * flux, axis=0, keepdims=True)
        cross_rhs = left_terms(weighted * SCALE).astype(jnp.bfloat16)
        norm_rhs = left_terms(weight).astype(jnp.bfloat16)

        def gain(rows):
            cross = dot(lin[rows, :], cross_rhs)
            norm = dot(sqr[rows, :], norm_rhs)
            return cross * cross * pl.reciprocal(norm, approx=True)

        def sums(rows, expo):
            out = [folded(expo)]
            for i in range(3):
                coord = crd[i, rows, :]
                out.append(folded(expo * jnp.concatenate([coord] * (block // 128), axis=1)))
            return out

        def finish(acc, shift):
            total, *moments = [jnp.sum(x, axis=0, keepdims=True) for x in acc]
            for i in range(3):
                means_ref[i, pl.ds(row, 1), lanes] = moments[i] / total
            evidence_ref[pl.ds(row, 1), lanes] = (shift * math.log(2.0) - half) + jnp.log(total)

        blank = jnp.zeros((8, block), jnp.float32)
        small = jnp.max(half) <= SAFE * math.log(2.0)

        @pl.when(small)
        def _():
            acc = [blank] * 4
            for start in range(0, ntmpl, chunk):
                rows = pl.ds(start, chunk)
                acc = [a + b for a, b in zip(acc, sums(rows, jnp.exp2(gain(rows))))]
            finish(acc, jnp.zeros_like(half))

        @pl.when(jnp.logical_not(small))
        def _():
            def step(i, carry):
                peak, *acc = carry
                rows = pl.ds(pl.multiple_of(i * chunk, chunk), chunk)
                values = gain(rows)
                later = jnp.maximum(peak, jnp.max(values, axis=0, keepdims=True))
                fade = jnp.exp2(peak - later)
                terms = sums(rows, jnp.exp2(values - later))
                return (later, *(a * fade + b for a, b in zip(acc, terms)))

            peak, *acc = lax.fori_loop(0, ntmpl // chunk, step, (jnp.zeros_like(half), *[blank] * 4))
            finish(acc, peak)

        return 0

    lax.fori_loop(0, height * (cols // block), one_block, 0)


def fit_pixels(flux, weight, bank, index):
    height, _, cols = flux.shape
    ntmpl = bank.shape[1]
    block = math.gcd(cols, 256)
    chunk = math.gcd(ntmpl, 256)
    vmem = pl.BlockSpec(memory_space=pltpu.VMEM)
    return pl.pallas_call(
        lambda *refs: fit_kernel(block, chunk, *refs),
        in_specs=[vmem] * 4,
        out_specs=[vmem] * 2,
        out_shape=[
            jax.ShapeDtypeStruct((3, height, cols), jnp.float32),
            jax.ShapeDtypeStruct((height, cols), jnp.float32),
        ],
        scratch_shapes=[
            pltpu.VMEM((ntmpl, 8 * PIECE), jnp.bfloat16),
            pltpu.VMEM((ntmpl, 8 * PIECE), jnp.bfloat16),
            pltpu.VMEM((3, ntmpl, 128), jnp.float32),
        ],
        compiler_params=pltpu.CompilerParams(vmem_limit_bytes=40 * 2**20),
    )(bank, index, flux, weight)


def body(sky_image, inverse_var, kernel_taps, kernel_sizes, templates, grid_index):
    radius = (kernel_taps.shape[1] - 1) // 2
    taps = kernel_table(kernel_taps, kernel_sizes, radius)
    flux, weight, bank, index = prepare(taps, sky_image, inverse_var, templates, grid_index)
    means, evidence = fit_pixels(flux, weight, bank, index)
    return means, evidence


def solution(mesh):
    placed = (
        P(None, "tile", None),
        P(None, "tile", None),
        P(),
        P(),
        P(None, "tmpl"),
        P(None, "tmpl"),
    )
    return jax.shard_map(
        body,
        mesh=mesh,
        in_specs=placed,
        out_specs=(P(None, "tile", "tmpl"), P("tile", "tmpl")),
        check_vma=False,
    )
```

time: 273 us -> 112 us (0.41)
  the two profiles are of different devices: /device:TPU:20 before, /device:TPU:17 now
where the time goes in v2:
time: 112 us; the launch traced here: 111 us
  Pallas kernels  105 us (94%)
  local copies, waits for them, and re-layouts  4.09 us (4%)
  other arithmetic  1.67 us (1%)
    pallas_call x1, Pallas kernels, fit_pixels(): pl.pallas_call(lambda *refs: fit_kernel(block, chunk, *refs), in_specs=[v...  92.8 us
    pallas_call x1, Pallas kernels, prepare(): pl.pallas_call(prep_kernel, in_specs=[pl.BlockSpec(memory_space=pltpu.SME...  12 us
    unnamed x8, local copies, waits for them, and re-layouts  4.09 us

profile of v2, /device:TPU:17, one launch (start us, length us, event | category | flops | bytes accessed | tf_op | source)
XLA Modules:
  0.0 111.2 jit_solution(8062220742101375876)
XLA Ops:
  0.6 0.9 fusion.1
  1.5 0.8 fusion.taps
  2.3 0.0 copy-start
  2.3 1.3 %copy-done = f32[10,16,2048]{2,1,0:T(8,128)S(1)} copy-done((f32[10,16,2048]{2,1,0:T(8,128)S(1)}, f32[10,16,2048]{2,1,0:T(8,128)}, u32[]{:S(2)}) %copy-start) | copy-done | bytes 1310744
  3.6 0.0 copy-start.1
  3.6 1.3 %copy-done.1 = f32[10,16,2048]{2,1,0:T(8,128)S(1)} copy-done((f32[10,16,2048]{2,1,0:T(8,128)S(1)}, f32[10,16,2048]{2,1,0:T(8,128)}, u32[]{:S(2)}) %copy-start.1) | copy-done | bytes 1310744
  4.9 0.0 copy-start.2
  4.9 0.8 copy-done.2
  5.7 0.0 copy-start.3
  5.7 0.7 copy-done.3
  6.4 12.0 %shard_map.77 = (f32[16,16,512]{2,1,0:T(8,128)S(1)}, f32[16,16,512]{2,1,0:T(8,128)S(1)}, f32[10,2048]{1,0:T(8,128)S(1)}, s32[3,2048]{1,0:T(4,128)S(1)}) custom-call(f32[10,17]{1,0:T(8,128)S(1)} %fusion.taps, f32[10,16,2048]{2,1,0:T(8,128)S(1)} %copy-done, f32[10,16,2048]{2,1,0:T(8,128)S(1)} %copy-done.1, f32[10,512]{1,0:T(8,128)S(1)} %copy-done.2, ...), custom_call_target="tpu_custom_call" | custom-call | tf_op jit(solution)/shard_map/pallas_call | solution.py:196
  18.4 92.8 %shard_map.78 = (f32[3,16,512]{2,1,0:T(8,128)}, f32[16,512]{1,0:T(8,128)}) custom-call(f32[10,2048]{1,0:T(8,128)S(1)} %get-tuple-element.6.refs_0_, s32[3,2048]{1,0:T(4,128)S(1)} %get-tuple-element.7.refs_1_, f32[16,16,512]{2,1,0:T(8,128)S(1)} %get-tuple-element.8.refs_2_, f32[16,16,512]{2,1,0:T(8,128)S(1)} %get-tuple-element.9.refs_3_), custom_call_target="tpu_custom_call" | custom-call | tf_op jit(solution)/shard_map/pallas_call | solution.py:324
  (1 shorter events, 0.0 us)
Async XLA Ops:
  2.3 1.3 %copy-start = (f32[10,16,2048]{2,1,0:T(8,128)S(1)}, f32[10,16,2048]{2,1,0:T(8,128)}, u32[]{:S(2)}) copy-start(f32[10,16,2048]{2,1,0:T(8,128)} %sky.1) | copy-start | bytes 3932164
  3.6 1.3 %copy-start.1 = (f32[10,16,2048]{2,1,0:T(8,128)S(1)}, f32[10,16,2048]{2,1,0:T(8,128)}, u32[]{:S(2)}) copy-start(f32[10,16,2048]{2,1,0:T(8,128)} %inverse_var.1) | copy-start | bytes 3932164
  4.9 0.8 copy-start.2
  5.7 0.7 copy-start.3

commit v3 on v2

--- a/solution.py
+++ b/solution.py
@@ -10,24 +10,17 @@
 GRID = 64
 PIECE = 16
 SCALE = math.sqrt(0.5 * math.log2(math.e))
-SAFE = 100.0
+SAFE = 69.0
 
 
 MESH = pl.DeviceIdType.MESH
 
 
-def kernel_table(kernel_taps, kernel_sizes, radius):
-    offsets = jnp.arange(2 * radius + 1, dtype=jnp.int32) - radius
-    inside = jnp.abs(offsets)[None, :] <= kernel_sizes[:, None]
-    masked = jnp.where(inside, kernel_taps, jnp.float32(0.0))
-    return masked / jnp.sum(masked, axis=1, keepdims=True)
-
-
 def prep_kernel(
-    taps, sky, inverse_var, templates, grid_index,
+    taps, sizes, sky, inverse_var, templates, grid_index,
     flux_out, weight_out, bank, index,
     win, weight, left, right, smooth,
-    local_sem, side_sem, send_sem, recv_sem, bank_send, bank_recv,
+    local_sem, side_sem, keep_sem, send_sem, recv_sem, bank_send, bank_recv,
 ):
     bands, height, _ = sky.shape
     radius = (taps.shape[1] - 1) // 2
@@ -52,6 +45,11 @@
     before.start()
     after.start()
     weights.start()
+    mine = pl.ds(pl.multiple_of(me * held, 128), held)
+    keep_bank = pltpu.make_async_copy(templates, bank.at[:, mine], keep_sem.at[0])
+    keep_index = pltpu.make_async_copy(grid_index, index.at[:, mine], keep_sem.at[1])
+    keep_bank.start()
+    keep_index.start()
 
     barrier = pltpu.get_barrier_semaphore()
     peers = [lax.rem(me + s, shards) for s in range(1, shards)]
@@ -104,7 +102,6 @@
     def _():
         up.start()
 
-    mine = pl.ds(pl.multiple_of(me * held, 128), held)
     copies = []
     for s, peer in enumerate(peers):
         for which, (source, target) in enumerate(((templates, bank), (grid_index, index))):
@@ -118,20 +115,25 @@
             )
             copy.start()
             copies.append(copy)
-    bank[:, mine] = templates[...]
-    index[:, mine] = grid_index[...]
-
-    def along_cols(band, rows):
+
+    def taps_of(band):
+        size = sizes[band]
+        return [
+            jnp.where(abs(t - radius) <= size, taps[band, t], jnp.float32(0.0))
+            for t in range(2 * radius + 1)
+        ]
+
+    def along_cols(band, rows, tap):
         part = win[band, rows, :]
-        total = taps[band, radius] * part[:, :cols]
+        total = tap[radius] * part[:, :cols]
         for t in range(2 * radius + 1):
             if t != radius:
                 moved = pltpu.roll(part, (radius - t) % (cols + edge), 1)
-                total = total + taps[band, t] * moved[:, :cols]
+                total = total + tap[t] * moved[:, :cols]
         smooth[band, rows, :] = total
 
     def own_rows(band, _):
-        along_cols(band, inner)
+        along_cols(band, inner, taps_of(band))
         return 0
 
     lax.fori_loop(0, bands, own_rows, 0)
@@ -161,16 +163,20 @@
         win[:, pl.ds(height + radius, radius), :] = zero_rows
 
     def halo_rows(band, _):
-        along_cols(band, pl.ds(0, radius))
-        along_cols(band, pl.ds(height + radius, radius))
+        tap = taps_of(band)
+        along_cols(band, pl.ds(0, radius), tap)
+        along_cols(band, pl.ds(height + radius, radius), tap)
         return 0
 
     lax.fori_loop(0, bands, halo_rows, 0)
     for band in range(bands):
-        total = taps[band, 0] * smooth[band, pl.ds(0, height), :]
+        tap = taps_of(band)
+        total = tap[0] * smooth[band, pl.ds(0, height), :]
+        norm = tap[0]
         for t in range(1, 2 * radius + 1):
-            total = total + taps[band, t] * smooth[band, pl.ds(t, height), :]
-        flux_out[:, band, :] = total
+            total = total + tap[t] * smooth[band, pl.ds(t, height), :]
+            norm = norm + tap[t]
+        flux_out[:, band, :] = total / jnp.full((height, cols), norm * norm, jnp.float32)
 
     @pl.when(tile < tiles - 1)
     def _():
@@ -182,9 +188,11 @@
 
     for copy in copies:
         copy.wait()
-
-
-def prepare(taps, sky, inverse_var, templates, grid_index):
+    keep_bank.wait()
+    keep_index.wait()
+
+
+def prepare(taps, sizes, sky, inverse_var, templates, grid_index):
     bands, height, width = sky.shape
     radius = (taps.shape[1] - 1) // 2
     shards = lax.axis_size("tmpl")
@@ -195,7 +203,7 @@
     rows = height + 2 * radius
     return pl.pallas_call(
         prep_kernel,
-        in_specs=[pl.BlockSpec(memory_space=pltpu.SMEM), anywhere, anywhere, vmem, vmem],
+        in_specs=[pl.BlockSpec(memory_space=pltpu.SMEM)] * 2 + [anywhere] * 4,
         out_specs=[vmem] * 4,
         out_shape=[
             jax.ShapeDtypeStruct((height, PIECE, cols), jnp.float32),
@@ -213,13 +221,14 @@
             pltpu.SemaphoreType.DMA((2,)),
             pltpu.SemaphoreType.DMA((2,)),
             pltpu.SemaphoreType.DMA((2,)),
+            pltpu.SemaphoreType.DMA((2,)),
             pltpu.SemaphoreType.DMA((2, max(shards - 1, 1))),
             pltpu.SemaphoreType.DMA((2, max(shards - 1, 1))),
         ],
         compiler_params=pltpu.CompilerParams(
-            collective_id=0, has_side_effects=True, vmem_limit_bytes=32 * 2**20
+            collective_id=0, has_side_effects=True, vmem_limit_bytes=56 * 2**20
         ),
-    )(taps, sky, inverse_var, templates, grid_index)
+    )(taps, sizes, sky, inverse_var, templates, grid_index)
 
 
 def split3(x):
@@ -244,9 +253,13 @@
     return lax.dot_general(a, b, (((1,), (0,)), ((), ())), preferred_element_type=jnp.float32)
 
 
-def fit_kernel(block, chunk, bank_ref, index_ref, flux_ref, weight_ref, means_ref, evidence_ref, lin, sqr, crd):
+def fit_kernel(
+    block, chunk, slab, bank_ref, index_ref, flux_ref, weight_ref,
+    means_ref, evidence_ref, lin, sqr, crd, cross_a, norm_a, cross_b, norm_b,
+):
     bands, ntmpl = bank_ref.shape
     height, _, cols = flux_ref.shape
+    steps = height * (cols // block)
     bank = jnp.concatenate([bank_ref[...], jnp.zeros((PIECE - bands, ntmpl), jnp.float32)], axis=0)
     lin[...] = right_terms(bank).T.astype(jnp.bfloat16)
     sqr[...] = right_terms(bank * bank).T.astype(jnp.bfloat16)
@@ -255,74 +268,106 @@
     for i in range(3):
         crd[i] = jnp.broadcast_to(coords[:, i : i + 1], (ntmpl, 128))
 
+    def place(step):
+        row = step // (cols // block)
+        return row, pl.ds(pl.multiple_of(lax.rem(step, cols // block) * block, block), block)
+
+    def sides(step):
+        row, lanes = place(step)
+        flux, weight = flux_ref[row, :, lanes], weight_ref[row, :, lanes]
+        return (
+            left_terms(weight * flux * SCALE).astype(jnp.bfloat16),
+            left_terms(weight).astype(jnp.bfloat16),
+        )
+
+    def half_of(step):
+        row, lanes = place(step)
+        flux, weight = flux_ref[row, :, lanes], weight_ref[row, :, lanes]
+        return 0.5 * jnp.sum(weight * flux * flux, axis=0, keepdims=True)
+
     def folded(x):
         return jnp.sum(x.reshape(x.shape[0] // 8, 8, x.shape[1]), axis=0)
 
-    def one_block(step, _):
-        row = step // (cols // block)
-        lanes = pl.ds(pl.multiple_of(lax.rem(step, cols // block) * block, block), block)
-        flux, weight = flux_ref[row, :, lanes], weight_ref[row, :, lanes]
-        weighted = weight * flux
-        half = 0.5 * jnp.sum(weighted * flux, axis=0, keepdims=True)
-        cross_rhs = left_terms(weighted * SCALE).astype(jnp.bfloat16)
-        norm_rhs = left_terms(weight).astype(jnp.bfloat16)
-
-        def gain(rows):
-            cross = dot(lin[rows, :], cross_rhs)
-            norm = dot(sqr[rows, :], norm_rhs)
-            return cross * cross * pl.reciprocal(norm, approx=True)
-
-        def sums(rows, expo):
-            out = [folded(expo)]
-            for i in range(3):
-                coord = crd[i, rows, :]
-                out.append(folded(expo * jnp.concatenate([coord] * (block // 128), axis=1)))
-            return out
-
-        def finish(acc, shift):
-            total, *moments = [jnp.sum(x, axis=0, keepdims=True) for x in acc]
-            for i in range(3):
-                means_ref[i, pl.ds(row, 1), lanes] = moments[i] / total
-            evidence_ref[pl.ds(row, 1), lanes] = (shift * math.log(2.0) - half) + jnp.log(total)
-
-        blank = jnp.zeros((8, block), jnp.float32)
-        small = jnp.max(half) <= SAFE * math.log(2.0)
-
-        @pl.when(small)
-        def _():
-            acc = [blank] * 4
-            for start in range(0, ntmpl, chunk):
-                rows = pl.ds(start, chunk)
-                acc = [a + b for a, b in zip(acc, sums(rows, jnp.exp2(gain(rows))))]
-            finish(acc, jnp.zeros_like(half))
-
-        @pl.when(jnp.logical_not(small))
-        def _():
-            def step(i, carry):
+    def sums(acc, rows, expo):
+        out = [acc[0] + folded(expo)]
+        for i in range(3):
+            coord = crd[i, rows, :]
+            out.append(acc[i + 1] + folded(expo * jnp.concatenate([coord] * (block // 128), axis=1)))
+        return out
+
+    def finish(step, acc, shift):
+        row, lanes = place(step)
+        total, *moments = [jnp.sum(x, axis=0, keepdims=True) for x in acc]
+        for i in range(3):
+            means_ref[i, pl.ds(row, 1), lanes] = moments[i] / total
+        evidence_ref[pl.ds(row, 1), lanes] = (shift * math.log(2.0) - half_of(step)) + jnp.log(total)
+
+    blank = jnp.zeros((8, block), jnp.float32)
+    bound = 0.5 * jnp.sum(weight_ref[...] * flux_ref[...] * flux_ref[...], axis=1)
+    small = jnp.max(bound) <= SAFE
+
+    def products(cross_rhs, norm_rhs, rows, cross, norm):
+        cross[rows, :] = dot(lin[rows, :], cross_rhs)
+        norm[rows, :] = dot(sqr[rows, :], norm_rhs)
+
+    def both(step, now, ahead):
+        if ahead is not None:
+            rhs = sides(lax.rem(step + 1, steps))
+        acc = [blank] * 4
+        for start in range(0, ntmpl, chunk):
+            if ahead is not None:
+                products(*rhs, pl.ds(start, chunk), *ahead)
+            for at in range(start, start + chunk, slab):
+                rows = pl.ds(at, slab)
+                cross = now[0][rows, :]
+                gain = cross * cross * pl.reciprocal(now[1][rows, :], approx=True)
+                acc = sums(acc, rows, jnp.exp2(gain))
+        finish(step, acc, 0.0)
+
+    @pl.when(small)
+    def _():
+        first, second = (cross_a, norm_a), (cross_b, norm_b)
+        products(*sides(0), pl.ds(0, ntmpl), *first)
+
+        def pair(i, _):
+            both(2 * i, first, second)
+            both(2 * i + 1, second, first)
+            return 0
+
+        lax.fori_loop(0, steps // 2, pair, 0)
+        if steps % 2:
+            both(steps - 1, first, None)
+
+    @pl.when(jnp.logical_not(small))
+    def _():
+        def one(step, _):
+            rhs = sides(step)
+
+            def part(i, carry):
                 peak, *acc = carry
-                rows = pl.ds(pl.multiple_of(i * chunk, chunk), chunk)
-                values = gain(rows)
+                rows = pl.ds(pl.multiple_of(i * slab, slab), slab)
+                cross = dot(lin[rows, :], rhs[0])
+                values = cross * cross * pl.reciprocal(dot(sqr[rows, :], rhs[1]), approx=True)
                 later = jnp.maximum(peak, jnp.max(values, axis=0, keepdims=True))
                 fade = jnp.exp2(peak - later)
-                terms = sums(rows, jnp.exp2(values - later))
-                return (later, *(a * fade + b for a, b in zip(acc, terms)))
-
-            peak, *acc = lax.fori_loop(0, ntmpl // chunk, step, (jnp.zeros_like(half), *[blank] * 4))
-            finish(acc, peak)
-
-        return 0
-
-    lax.fori_loop(0, height * (cols // block), one_block, 0)
+                return (later, *sums([a * fade for a in acc], rows, jnp.exp2(values - later)))
+
+            peak, *acc = lax.fori_loop(0, ntmpl // slab, part, (jnp.zeros((1, block), jnp.float32), *[blank] * 4))
+            finish(step, acc, peak)
+            return 0
+
+        lax.fori_loop(0, steps, one, 0)
 
 
 def fit_pixels(flux, weight, bank, index):
     height, _, cols = flux.shape
     ntmpl = bank.shape[1]
     block = math.gcd(cols, 256)
-    chunk = math.gcd(ntmpl, 256)
+    chunk = math.gcd(ntmpl, 512)
+    slab = math.gcd(chunk, 64)
     vmem = pl.BlockSpec(memory_space=pltpu.VMEM)
     return pl.pallas_call(
-        lambda *refs: fit_kernel(block, chunk, *refs),
+        lambda *refs: fit_kernel(block, chunk, slab, *refs),
         in_specs=[vmem] * 4,
         out_specs=[vmem] * 2,
         out_shape=[
@@ -333,15 +378,16 @@
             pltpu.VMEM((ntmpl, 8 * PIECE), jnp.bfloat16),
             pltpu.VMEM((ntmpl, 8 * PIECE), jnp.bfloat16),
             pltpu.VMEM((3, ntmpl, 128), jnp.float32),
-        ],
+        ]
+        + [pltpu.VMEM((ntmpl, block), jnp.float32)] * 4,
         compiler_params=pltpu.CompilerParams(vmem_limit_bytes=40 * 2**20),
     )(bank, index, flux, weight)
 
 
 def body(sky_image, inverse_var, kernel_taps, kernel_sizes, templates, grid_index):
-    radius = (kernel_taps.shape[1] - 1) // 2
-    taps = kernel_table(kernel_taps, kernel_sizes, radius)
-    flux, weight, bank, index = prepare(taps, sky_image, inverse_var, templates, grid_index)
+    flux, weight, bank, index = prepare(
+        kernel_taps, kernel_sizes, sky_image, inverse_var, templates, grid_index
+    )
     means, evidence = fit_pixels(flux, weight, bank, index)
     return means, evidence
 

time: 112 us -> 220 us (1.96)
  the two profiles are of different devices: /device:TPU:17 before, /device:TPU:20 now
where the time goes in v3:
time: 220 us; the launch traced here: 217 us
  Pallas kernels  213 us (97%)
  local copies, waits for them, and re-layouts  3.74 us (2%)
    pallas_call x1, Pallas kernels, fit_pixels(): pl.pallas_call(lambda *refs: fit_kernel(block, chunk, slab, *refs), in_sp...  202 us
    pallas_call x1, Pallas kernels, prepare(): pl.pallas_call(prep_kernel, in_specs=[pl.BlockSpec(memory_space=pltpu.SME...  10.7 us

profile of v3, /device:TPU:20, one launch (start us, length us, event | category | flops | bytes accessed | tf_op | source)
XLA Modules:
  0.0 217.0 jit_solution(141336409665132561)
XLA Ops:
  0.6 10.7 %shard_map.77 = (f32[16,16,512]{2,1,0:T(8,128)}, f32[16,16,512]{2,1,0:T(8,128)}, f32[10,2048]{1,0:T(8,128)}, s32[3,2048]{1,0:T(4,128)}) custom-call(f32[10,17]{1,0:T(8,128)} %taps.1, s32[10]{0:T(128)} %sizes.1, f32[10,16,2048]{2,1,0:T(8,128)} %sky.1, f32[10,16,2048]{2,1,0:T(8,128)} %inverse_var.1, f32[10,512]{1,0:T(8,128)} %templates.1, s32[3,512]{1,0:T(4,128)} %grid_index.1), custom_call_target="tpu_custom_call" | custom-call | tf_op jit(solution)/shard_map/pallas_call | solution.py:204
  11.3 0.0 copy-start
  11.3 1.0 copy-done
  12.4 0.0 copy-start.1
  12.4 1.0 copy-done.1
  13.4 0.0 copy-start.2
  13.4 0.9 copy-done.2
  14.3 0.0 copy-start.3
  14.3 0.8 copy-done.3
  15.1 201.9 %shard_map.78 = (f32[3,16,512]{2,1,0:T(8,128)}, f32[16,512]{1,0:T(8,128)}) custom-call(f32[10,2048]{1,0:T(8,128)S(1)} %copy-done.2, s32[3,2048]{1,0:T(4,128)S(1)} %copy-done.3, f32[16,16,512]{2,1,0:T(8,128)S(1)} %copy-done, f32[16,16,512]{2,1,0:T(8,128)S(1)} %copy-done.1), custom_call_target="tpu_custom_call" | custom-call | tf_op jit(solution)/shard_map/pallas_call | solution.py:369
Async XLA Ops:
  11.3 1.0 copy-start
  12.4 1.0 copy-start.1
  13.4 0.9 copy-start.2
  14.3 0.8 copy-start.3

commit v4 on v3

--- a/solution.py
+++ b/solution.py
@@ -254,9 +254,16 @@
 
 
 def fit_kernel(
-    block, chunk, slab, bank_ref, index_ref, flux_ref, weight_ref,
-    means_ref, evidence_ref, lin, sqr, crd, cross_a, norm_a, cross_b, norm_b,
+    block, chunk, slab, bank_in, index_in, flux_in, weight_in,
+    means_ref, evidence_ref, bank_ref, index_ref, flux_ref, weight_ref, sem,
+    lin, sqr, crd, cross_a, norm_a, cross_b, norm_b,
 ):
+    pairs = ((bank_in, bank_ref), (index_in, index_ref), (flux_in, flux_ref), (weight_in, weight_ref))
+    fetches = [pltpu.make_async_copy(*pair, sem.at[i]) for i, pair in enumerate(pairs)]
+    for fetch in fetches:
+        fetch.start()
+    fetches[0].wait()
+    fetches[1].wait()
     bands, ntmpl = bank_ref.shape
     height, _, cols = flux_ref.shape
     steps = height * (cols // block)
@@ -268,6 +275,9 @@
     for i in range(3):
         crd[i] = jnp.broadcast_to(coords[:, i : i + 1], (ntmpl, 128))
 
+    fetches[2].wait()
+    fetches[3].wait()
+
     def place(step):
         row = step // (cols // block)
         return row, pl.ds(pl.multiple_of(lax.rem(step, cols // block) * block, block), block)
@@ -319,9 +329,11 @@
                 products(*rhs, pl.ds(start, chunk), *ahead)
             for at in range(start, start + chunk, slab):
                 rows = pl.ds(at, slab)
-                cross = now[0][rows, :]
-                gain = cross * cross * pl.reciprocal(now[1][rows, :], approx=True)
-                acc = sums(acc, rows, jnp.exp2(gain))
+                cross, norm = now[0][rows, :], now[1][rows, :]
+                upper, lower = norm[: slab // 2], norm[slab // 2 :]
+                shared = pl.reciprocal(upper * lower, approx=True)
+                inverse = jnp.concatenate([shared * lower, shared * upper], axis=0)
+                acc = sums(acc, rows, jnp.exp2(cross * cross * inverse))
         finish(step, acc, 0.0)
 
     @pl.when(small)
@@ -364,23 +376,26 @@
     ntmpl = bank.shape[1]
     block = math.gcd(cols, 256)
     chunk = math.gcd(ntmpl, 512)
-    slab = math.gcd(chunk, 64)
+    slab = math.gcd(chunk, 32)
+    anywhere = pl.BlockSpec(memory_space=pl.ANY)
     vmem = pl.BlockSpec(memory_space=pltpu.VMEM)
     return pl.pallas_call(
         lambda *refs: fit_kernel(block, chunk, slab, *refs),
-        in_specs=[vmem] * 4,
+        in_specs=[anywhere] * 4,
         out_specs=[vmem] * 2,
         out_shape=[
             jax.ShapeDtypeStruct((3, height, cols), jnp.float32),
             jax.ShapeDtypeStruct((height, cols), jnp.float32),
         ],
-        scratch_shapes=[
+        scratch_shapes=[pltpu.VMEM(x.shape, x.dtype) for x in (bank, index, flux, weight)]
+        + [
+            pltpu.SemaphoreType.DMA((4,)),
             pltpu.VMEM((ntmpl, 8 * PIECE), jnp.bfloat16),
             pltpu.VMEM((ntmpl, 8 * PIECE), jnp.bfloat16),
             pltpu.VMEM((3, ntmpl, 128), jnp.float32),
         ]
         + [pltpu.VMEM((ntmpl, block), jnp.float32)] * 4,
-        compiler_params=pltpu.CompilerParams(vmem_limit_bytes=40 * 2**20),
+        compiler_params=pltpu.CompilerParams(vmem_limit_bytes=56 * 2**20),
     )(bank, index, flux, weight)
 
 

time: 220 us -> 368 us (1.67)
  Pallas kernels: 213 us -> 364 us
  local copies, waits for them, and re-layouts: 3.74 us -> 0 us
    pallas_call x1, Pallas kernels: 202 us -> 354 us  [fit_pixels(): pl.pallas_call(lambda *refs: fit_kernel(block, chunk, slab, *refs), in_sp...]
    unnamed x8 -> x0, local copies, waits for them, and re-layouts: 3.74 us -> none
where the time goes in v4:
time: 368 us; the launch traced here: 365 us
  Pallas kernels  364 us (99%)
    pallas_call x1, Pallas kernels, fit_pixels(): pl.pallas_call(lambda *refs: fit_kernel(block, chunk, slab, *refs), in_sp...  354 us
    pallas_call x1, Pallas kernels, prepare(): pl.pallas_call(prep_kernel, in_specs=[pl.BlockSpec(memory_space=pltpu.SME...  10.7 us

profile of v4, /device:TPU:20, one launch (start us, length us, event | category | flops | bytes accessed | tf_op | source)
XLA Modules:
  0.0 365.0 jit_solution(1829529739872364530)
XLA Ops:
  0.6 10.7 %shard_map.77 = (f32[16,16,512]{2,1,0:T(8,128)}, f32[16,16,512]{2,1,0:T(8,128)}, f32[10,2048]{1,0:T(8,128)}, s32[3,2048]{1,0:T(4,128)}) custom-call(f32[10,17]{1,0:T(8,128)} %taps.1, s32[10]{0:T(128)} %sizes.1, f32[10,16,2048]{2,1,0:T(8,128)} %sky.1, f32[10,16,2048]{2,1,0:T(8,128)} %inverse_var.1, f32[10,512]{1,0:T(8,128)} %templates.1, s32[3,512]{1,0:T(4,128)} %grid_index.1), custom_call_target="tpu_custom_call" | custom-call | tf_op jit(solution)/shard_map/pallas_call | solution.py:204
  11.3 353.7 %shard_map.78 = (f32[3,16,512]{2,1,0:T(8,128)}, f32[16,512]{1,0:T(8,128)}) custom-call(f32[10,2048]{1,0:T(8,128)} %get-tuple-element.6.refs_0_, s32[3,2048]{1,0:T(4,128)} %get-tuple-element.7.refs_1_, f32[16,16,512]{2,1,0:T(8,128)} %get-tuple-element.8.refs_2_, f32[16,16,512]{2,1,0:T(8,128)} %get-tuple-element.9.refs_3_), custom_call_target="tpu_custom_call" | custom-call | tf_op jit(solution)/shard_map/pallas_call | solution.py:382

commit v5 on v4

--- a/solution.py
+++ b/solution.py
@@ -374,9 +374,9 @@
 def fit_pixels(flux, weight, bank, index):
     height, _, cols = flux.shape
     ntmpl = bank.shape[1]
-    block = math.gcd(cols, 256)
+    block = math.gcd(cols, 512)
     chunk = math.gcd(ntmpl, 512)
-    slab = math.gcd(chunk, 32)
+    slab = math.gcd(chunk, 16)
     anywhere = pl.BlockSpec(memory_space=pl.ANY)
     vmem = pl.BlockSpec(memory_space=pltpu.VMEM)
     return pl.pallas_call(

time: 368 us -> 399 us (1.084)
  Pallas kernels: 364 us -> 396 us
    pallas_call x1, Pallas kernels: 354 us -> 385 us  [fit_pixels(): pl.pallas_call(lambda *refs: fit_kernel(block, chunk, slab, *refs), in_sp...]
where the time goes in v5:
time: 399 us; the launch traced here: 397 us
  Pallas kernels  396 us (99%)
    pallas_call x1, Pallas kernels, fit_pixels(): pl.pallas_call(lambda *refs: fit_kernel(block, chunk, slab, *refs), in_sp...  385 us
    pallas_call x1, Pallas kernels, prepare(): pl.pallas_call(prep_kernel, in_specs=[pl.BlockSpec(memory_space=pltpu.SME...  10.7 us

profile of v5, /device:TPU:20, one launch (start us, length us, event | category | flops | bytes accessed | tf_op | source)
XLA Modules:
  0.0 396.6 jit_solution(17954050088678892893)
XLA Ops:
  0.6 10.7 %shard_map.77 = (f32[16,16,512]{2,1,0:T(8,128)}, f32[16,16,512]{2,1,0:T(8,128)}, f32[10,2048]{1,0:T(8,128)}, s32[3,2048]{1,0:T(4,128)}) custom-call(f32[10,17]{1,0:T(8,128)} %taps.1, s32[10]{0:T(128)} %sizes.1, f32[10,16,2048]{2,1,0:T(8,128)} %sky.1, f32[10,16,2048]{2,1,0:T(8,128)} %inverse_var.1, f32[10,512]{1,0:T(8,128)} %templates.1, s32[3,512]{1,0:T(4,128)} %grid_index.1), custom_call_target="tpu_custom_call" | custom-call | tf_op jit(solution)/shard_map/pallas_call | solution.py:204
  11.3 385.3 %shard_map.78 = (f32[3,16,512]{2,1,0:T(8,128)}, f32[16,512]{1,0:T(8,128)}) custom-call(f32[10,2048]{1,0:T(8,128)} %get-tuple-element.6.refs_0_, s32[3,2048]{1,0:T(4,128)} %get-tuple-element.7.refs_1_, f32[16,16,512]{2,1,0:T(8,128)} %get-tuple-element.8.refs_2_, f32[16,16,512]{2,1,0:T(8,128)} %get-tuple-element.9.refs_3_), custom_call_target="tpu_custom_call" | custom-call | tf_op jit(solution)/shard_map/pallas_call | solution.py:382
